TPU v7x, 32 devices: a whole 2x2x4 slice. The times are simulated.
32 devices in a mesh: lat: 8 (over y, x, core), lon: 4 (over z).
Axes of the slice: x: 2, y: 2, z: 4, core: 2. Of those that a mesh axis runs over, the one named last changes fastest.
Arguments:
- field: bfloat16 [192, 384, 1440], P('lon', 'lat'), may hold values from -6 to 6
- cotangent: bfloat16 [192, 384, 1440], P('lon', 'lat'), may hold values from -6 to 6
- legendre: bfloat16 [384, 384, 384], P('lat', 'lon'), may hold values from -0.3125 to 0.3125
- spectral_weight: bfloat16 [384, 2, 192, 192], P('lon'), may hold values from -0.3125 to 0.3125
Outputs:
- output: bfloat16 [192, 384, 1440], P('lon', 'lat')
- field_grad: bfloat16 [192, 384, 1440], P('lon', 'lat')
- weight_grad: bfloat16 [384, 2, 192, 192], P('lon', None, 'lat')
All inputs are finite; a program needn't handle non-finite values.
Results may differ from a plain program's by a relative error of at most 0.018.
Values may be sent and summed in bfloat16 or wider, within the bound.
A program may use at most 192 MiB of HBM per device.

v0:
```python
import math

import jax
import jax.numpy as jnp
from jax import lax
from jax.sharding import PartitionSpec as P


def wave_table(longitudes, wavenumbers):
    wave_index = jnp.arange(wavenumbers, dtype=jnp.int32)[:, None]
    column = jnp.arange(longitudes, dtype=jnp.int32)[None, :]
    phase = (column * wave_index % longitudes).astype(jnp.float32) * (2.0 * math.pi / longitudes)
    factor = 1.0 / math.sqrt(longitudes)
    return jnp.stack([jnp.cos(phase) * factor, -jnp.sin(phase) * factor], axis=1).astype(
        jnp.bfloat16
    )


def batched_lat(waves, table):
    wavenumbers, parts, channels, latitudes = waves.shape
    flat = waves.reshape(wavenumbers, parts * channels, latitudes)
    result = lax.dot_general(
        table, flat, (((2,), (2,)), ((0,), (0,))), preferred_element_type=jnp.float32
    )
    rounded = result.astype(jnp.bfloat16).reshape(wavenumbers, table.shape[1], parts, channels)
    return jnp.transpose(rounded, (1, 0, 2, 3))


def batched_deg(spectrum, table):
    degrees, wavenumbers, parts, channels = spectrum.shape
    flat = spectrum.reshape(degrees, wavenumbers, parts * channels)
    result = lax.dot_general(
        flat, table, (((0,), (1,)), ((1,), (0,))), preferred_element_type=jnp.float32
    )
    return result.reshape(wavenumbers, parts, channels, table.shape[2])


def mix_forward(spectrum, weight):
    products = jnp.einsum("lmkc,ljdc->lmkjd", spectrum, weight, preferred_element_type=jnp.float32)
    real_out = products[:, :, 0, 0] - products[:, :, 1, 1]
    imag_out = products[:, :, 1, 0] + products[:, :, 0, 1]
    return jnp.stack([real_out, imag_out], axis=2).astype(jnp.bfloat16)


def mix_adjoint(grad_spec, weight):
    products = jnp.einsum("lmkd,ljdc->lmkjc", grad_spec, weight, preferred_element_type=jnp.float32)
    real_out = products[:, :, 0, 0] + products[:, :, 1, 1]
    imag_out = products[:, :, 1, 0] - products[:, :, 0, 1]
    return jnp.stack([real_out, imag_out], axis=2).astype(jnp.bfloat16)


def weight_term(grad_spec, spectrum):
    rotated = jnp.stack([grad_spec[:, :, 1], -grad_spec[:, :, 0]], axis=2)
    paired = jnp.stack([grad_spec, rotated], axis=3)
    return jnp.einsum(
        "lmkjd,lmkc->ljdc", paired, spectrum, preferred_element_type=jnp.float32
    ).astype(jnp.bfloat16)


def on_device(field, cotangent, legendre, spectral_weight):
    lat_count = lax.axis_size("lat")
    longitudes = field.shape[2]
    total_waves = legendre.shape[0] * lat_count
    fourier = wave_table(longitudes, total_waves)
    fourier_flat = fourier.reshape(2 * total_waves, longitudes)

    def to_waves(grid):
        channels, latitudes = (grid.shape[0], grid.shape[1])
        local_waves = lax.dot_general(
            fourier_flat,
            grid.reshape(channels * latitudes, longitudes),
            (((1,), (1,)), ((), ())),
            preferred_element_type=jnp.float32,
        )
        local_waves = local_waves.astype(jnp.bfloat16).reshape(total_waves, 2, channels, latitudes)
        return lax.all_to_all(local_waves, "lat", split_axis=0, concat_axis=3, tiled=True)

    def to_grid(waves):
        block_in = lax.all_to_all(waves, "lat", split_axis=3, concat_axis=0, tiled=True)
        wavenumbers, parts, channels, latitudes = block_in.shape
        flat = lax.dot_general(
            block_in.reshape(wavenumbers * parts, channels * latitudes),
            fourier_flat,
            (((0,), (0,)), ((), ())),
            preferred_element_type=jnp.float32,
        )
        return flat.reshape(channels, latitudes, longitudes)

    def legendre_forward(waves):
        return batched_lat(lax.all_gather(waves, "lon", axis=2, tiled=True), legendre)

    def legendre_inverse(spectrum):
        terms = batched_deg(spectrum, legendre)
        summed = lax.psum_scatter(
            terms.astype(jnp.bfloat16), "lon", scatter_dimension=2, tiled=True
        )
        return summed

    waves = to_waves(field)
    spectrum = legendre_forward(waves)
    mixed = mix_forward(spectrum, spectral_weight)
    back = legendre_inverse(mixed)
    output = (field.astype(jnp.float32) + to_grid(back)).astype(jnp.bfloat16)
    grad_waves = to_waves(cotangent)
    grad_spec = legendre_forward(grad_waves)
    grad_term = weight_term(grad_spec, spectrum)
    weight_grad = (
        lax.psum_scatter(grad_term, "lat", scatter_dimension=2, tiled=True)
        .astype(jnp.float32)
        .astype(jnp.bfloat16)
    )
    grad_mixed = mix_adjoint(grad_spec, spectral_weight)
    grad_back = legendre_inverse(grad_mixed)
    field_grad = (cotangent.astype(jnp.float32) + to_grid(grad_back)).astype(jnp.bfloat16)
    return (output, field_grad, weight_grad)


def solution(mesh):
    placed = (
        P("lon", "lat", None),
        P("lon", "lat", None),
        P("lat", "lon", None),
        P("lon", None, None, None),
    )
    return jax.shard_map(
        on_device,
        mesh=mesh,
        in_specs=placed,
        out_specs=(P("lon", "lat", None), P("lon", "lat", None), P("lon", None, "lat", None)),
        check_vma=False,
    )
```

profile of v0, /device:TPU:0, one launch (start us, length us, event | category | flops | bytes accessed | tf_op | source)
XLA Modules:
  0.0 1410.5 jit_solution(11325058508408172451)
XLA Ops:
  7.2 9.7 multiply_convert_fusion
  18.6 6.8 copy.102
  25.4 6.0 convert_element_type.98
  31.4 10.5 convolution_convert_fusion.3
  41.9 15.4 %reshape.210 = bf16[384,2,48,48]{3,2,1,0:T(8,128)(2,1)} reshape(bf16[768,2304]{1,0:T(8,128)(2,1)} %convolution_convert_fusion.3) | data formatting | bytes 7077888 | tf_op jit(solution)/shard_map/reshape | solution.py:75
  57.3 15.8 %reshape.229 = bf16[8,2,110592]{2,1,0:T(2,128)(2,1)} reshape(bf16[384,2,48,48]{3,2,1,0:T(8,128)(2,1)} %reshape.210) | data formatting | bytes 7077888
  73.1 47.3 %all_to_all.66 = bf16[8,2,110592]{2,1,0:T(2,128)(2,1)} all-to-all(bf16[8,2,110592]{2,1,0:T(2,128)(2,1)} %reshape.229), channel_id=1, replica_groups=mesh['lat'=8,'lon'=4] {'lat'}, dimensions={0} | all-to-all | bytes 7077888 | tf_op jit(solution)/shard_map/all_to_all | solution.py:76
  120.4 11.7 reshape.230
  132.1 18.3 %copy.103 = bf16[48,2,48,8,48]{4,3,2,1,0:T(8,128)(2,1)} copy(bf16[48,2,48,8,48]{4,2,1,0,3:T(8,128)(2,1)} %bitcast.144) | data formatting | bytes 7077888 | tf_op jit(solution)/shard_map/all_to_all | solution.py:76
  150.3 13.3 all_to_all.51
  163.7 10.5 convolution_convert_fusion.2
  174.3 15.5 %reshape.215 = bf16[384,2,48,48]{3,2,1,0:T(8,128)(2,1)} reshape(bf16[768,2304]{1,0:T(8,128)(2,1)} %convolution_convert_fusion.2) | data formatting | bytes 7077888 | tf_op jit(solution)/shard_map/reshape | solution.py:75
  189.7 15.8 %reshape.233 = bf16[8,2,110592]{2,1,0:T(2,128)(2,1)} reshape(bf16[384,2,48,48]{3,2,1,0:T(8,128)(2,1)} %reshape.215) | data formatting | bytes 7077888
  205.5 46.5 %all_to_all.67 = bf16[8,2,110592]{2,1,0:T(2,128)(2,1)} all-to-all(bf16[8,2,110592]{2,1,0:T(2,128)(2,1)} %reshape.233), channel_id=1, replica_groups=mesh['lat'=8,'lon'=4] {'lat'}, dimensions={0} | all-to-all | bytes 7077888 | tf_op jit(solution)/shard_map/all_to_all | solution.py:76
  252.0 11.6 reshape.234
  263.6 18.2 %copy.115 = bf16[48,2,48,8,48]{4,3,2,1,0:T(8,128)(2,1)} copy(bf16[48,2,48,8,48]{4,2,1,0,3:T(8,128)(2,1)} %bitcast.145) | data formatting | bytes 7077888 | tf_op jit(solution)/shard_map/all_to_all | solution.py:76
  281.9 13.4 all_to_all.58
  295.3 112.5 %all-gather.3.cloned.1.call-done = bf16[48,2,192,384]{3,2,1,0:T(8,128)(2,1)} async-done(((bf16[48,2,48,384]{3,2,1,0:T(8,128)(2,1)}), bf16[48,2,192,384]{3,2,1,0:T(8,128)(2,1)}) %all-gather.3.cloned.1.call-update) | async-done | bytes 14155792 | tf_op jit(solution)/shard_map/all_gather | solution.py:90
  407.8 9.0 convert_bitcast_fusion.1
  416.8 11.3 reshape.212
  428.1 17.7 %fusion.2 = f32[96,48,2,2,192]{4,1,3,2,0:T(8,128)} fusion(bf16[96,2,192,192]{3,2,1,0:T(8,128)(2,1)} %param.7, bf16[48,96,2,192]{3,2,1,0:T(2,128)(2,1)} %reshape.212), kind=kOutput, calls=%fused_computation.4 | convolution fusion | flops 1358954496 | bytes 31850496 | tf_op jit(solution)/shard_map/lmkc,ljdc->lmkjd/dot_general | solution.py:39
  445.8 4.6 fusion.20
  450.4 4.8 fusion.19
  455.2 3.1 pad_maximum_fusion
  458.3 9.3 copy.135
  467.7 10.4 reshape.225
  478.0 9.5 convolution_convert_fusion.1
  487.5 17.3 %copy.109 = bf16[48,2,192,384]{3,0,1,2:T(8,128)(2,1)} copy(bf16[48,2,192,384]{3,2,1,0:T(8,128)(2,1)} %bitcast.140) | data formatting | bytes 28311552 | tf_op jit(solution)/shard_map/convert_element_type | solution.py:95
  504.9 146.6 %all-gather.5.cloned.1.call-done = bf16[48,2,192,384]{3,2,1,0:T(8,128)(2,1)} async-done(((bf16[48,2,48,384]{3,2,1,0:T(8,128)(2,1)}), bf16[48,2,192,384]{3,2,1,0:T(8,128)(2,1)}) %all-gather.5.cloned.1.call-update) | async-done | bytes 14155792 | tf_op jit(solution)/shard_map/all_gather | solution.py:90
  651.5 9.0 convert_bitcast_fusion
  660.5 11.2 reshape.217
  671.6 19.1 %fusion = f32[96,48,2,2,192]{4,1,3,2,0:T(8,128)} fusion(bf16[96,2,192,192]{3,2,1,0:T(8,128)(2,1)} %param.7, bf16[48,96,2,192]{3,2,1,0:T(2,128)(2,1)} %reshape.217), kind=kOutput, calls=%fused_computation.2 | convolution fusion | flops 1358954496 | bytes 31850496 | tf_op jit(solution)/shard_map/lmkd,ljdc->lmkjc/dot_general | solution.py:46
  690.7 4.7 fusion.22
  695.4 4.6 fusion.21
  700.0 3.1 pad_maximum_fusion.1
  703.1 9.7 copy.139
  712.8 10.4 reshape.226
  723.2 9.5 convolution_convert_fusion
  732.7 17.1 %copy.121 = bf16[48,2,192,384]{3,0,1,2:T(8,128)(2,1)} copy(bf16[48,2,192,384]{3,2,1,0:T(8,128)(2,1)} %bitcast.141) | data formatting | bytes 28311552 | tf_op jit(solution)/shard_map/convert_element_type | solution.py:95
  750.0 7.5 copy.167
  760.8 13.4 bitcast_convert_fusion
  774.2 27.6 %copy.166 = bf16[96,2,192,192]{3,1,0,2:T(2,128)(2,1)} copy(bf16[96,2,192,192]{3,2,1,0:T(8,128)(2,1)} %bitcast_convert_fusion) | data formatting | bytes 28311552
  801.8 28.4 %reshape.227 = bf16[192,36864]{1,0:T(8,128)(2,1)} reshape(bf16[192,96,2,192]{3,2,1,0:T(2,128)(2,1)} %bitcast.139) | data formatting | bytes 28311552
  830.2 59.0 %reduce-scatter.6.cloned.1.call-done = bf16[48,2,48,384]{3,0,1,2:T(8,128)(2,1)} async-done(((bf16[48,2,192,384]{3,0,1,2:T(8,128)(2,1)}), bf16[48,2,48,384]{3,0,1,2:T(8,128)(2,1)}) %reduce-scatter.6.cloned.1.call-update) | async-done | bytes 3538960 | tf_op jit(solution)/shard_map/reduce_scatter | solution.py:94
  889.3 16.4 %copy.110 = bf16[48,2,48,384]{2,1,0,3:T(2,128)(2,1)} copy(bf16[48,2,48,384]{3,0,1,2:T(8,128)(2,1)} %reduce-scatter.6.cloned.1.call-done) | data formatting | bytes 7077888 | tf_op jit(solution)/shard_map/reduce_scatter | solution.py:94
  905.7 15.8 %reshape.231 = bf16[8,2,110592]{2,1,0:T(2,128)(2,1)} reshape(bf16[384,48,2,48]{3,2,1,0:T(2,128)(2,1)} %bitcast.146) | data formatting | bytes 7077888
  921.5 3.7 all-to-all-start.1
  925.2 204.6 %reduce-scatter.8.cloned.1.call-done = bf16[48,2,48,384]{3,0,1,2:T(8,128)(2,1)} async-done(((bf16[48,2,192,384]{3,0,1,2:T(8,128)(2,1)}), bf16[48,2,48,384]{3,0,1,2:T(8,128)(2,1)}) %reduce-scatter.8.cloned.1.call-update) | async-done | bytes 3538960 | tf_op jit(solution)/shard_map/reduce_scatter | solution.py:94
  1129.8 16.5 %copy.122 = bf16[48,2,48,384]{2,1,0,3:T(2,128)(2,1)} copy(bf16[48,2,48,384]{3,0,1,2:T(8,128)(2,1)} %reduce-scatter.8.cloned.1.call-done) | data formatting | bytes 7077888 | tf_op jit(solution)/shard_map/reduce_scatter | solution.py:94
  1146.3 16.1 %reshape.235 = bf16[8,2,110592]{2,1,0:T(2,128)(2,1)} reshape(bf16[384,48,2,48]{3,2,1,0:T(2,128)(2,1)} %bitcast.147) | data formatting | bytes 7077888
  1162.4 4.8 all-to-all-start.3
  1167.3 105.6 %reduce-scatter.10.cloned.1.call-done = bf16[24,36864]{1,0:T(8,128)(2,1)} async-done(((bf16[192,36864]{1,0:T(8,128)(2,1)}), bf16[24,36864]{1,0:T(8,128)(2,1)}) %reduce-scatter.10.cloned.1.call-update) | async-done | bytes 1769488
  1272.8 5.1 reshape.228
  1277.9 5.6 copy.144
  1283.5 10.5 reshape.232
  1294.1 22.0 %copy.137 = bf16[48,2,48,8,48]{4,2,1,0,3:T(8,128)(2,1)} copy(bf16[48,2,48,8,48]{2,1,0,4,3:T(2,128)(2,1)} %bitcast.148) | data formatting | bytes 7077888 | tf_op jit(solution)/shard_map/all_to_all | solution.py:79
  1316.0 12.5 reshape.213
  1328.6 3.6 copy.113
  1332.1 10.9 add_convert_fusion.1
  1343.0 11.5 reshape.236
  1354.6 22.0 %copy.141 = bf16[48,2,48,8,48]{4,2,1,0,3:T(8,128)(2,1)} copy(bf16[48,2,48,8,48]{2,1,0,4,3:T(2,128)(2,1)} %bitcast.150) | data formatting | bytes 7077888 | tf_op jit(solution)/shard_map/all_to_all | solution.py:79
  1376.5 12.5 reshape.218
  1389.1 3.6 copy.125
  1392.7 11.1 add_convert_fusion
  (24 shorter events, 5.3 us)
Async XLA Ops:
  7.2 400.6 %copy-start = (bf16[48,96,384]{2,1,0:T(8,128)(2,1)S(1)}, bf16[48,96,384]{2,1,0:T(8,128)(2,1)}, u32[]{:S(2)}) copy-start(bf16[48,96,384]{2,1,0:T(8,128)(2,1)} %param.6) | copy-start | bytes 10616836
  7.2 400.6 %all-gather.3.cloned.1.call-start = ((), (), s32[]{:S(2)}) async-start(), calls=%async_computation.7 | async-start | bytes 17694720 | tf_op jit(solution)/shard_map/all_gather | solution.py:90
  163.7 487.8 %all-gather.5.cloned.1.call-start = ((), (), s32[]{:S(2)}) async-start(), calls=%async_computation.9 | async-start | bytes 17694720 | tf_op jit(solution)/shard_map/all_gather | solution.py:90
  295.2 594.0 %reduce-scatter.6.cloned.1.call-start = ((), (), s32[]{:S(2)}) async-start(), calls=%async_computation.8 | async-start | bytes 17694720 | tf_op jit(solution)/shard_map/reduce_scatter | solution.py:94
  504.8 624.9 %reduce-scatter.8.cloned.1.call-start = ((), (), s32[]{:S(2)}) async-start(), calls=%async_computation.10 | async-start | bytes 17694720 | tf_op jit(solution)/shard_map/reduce_scatter | solution.py:94
  749.9 522.9 %reduce-scatter.10.cloned.1.call-start = ((), (), s32[]{:S(2)}) async-start(), calls=%async_computation.11 | async-start | bytes 15925248
  757.4 3.4 slice-start
  757.7 3.0 slice-start.1
  921.5 241.0 %all-to-all-start.1 = ((bf16[8,2,110592]{2,1,0:T(2,128)(2,1)}), bf16[8,2,110592]{2,1,0:T(2,128)(2,1)S(1)}, u32[]{:S(2)}, u32[]{:S(2)}) async-start(bf16[8,2,110592]{2,1,0:T(2,128)(2,1)} %reshape.231), calls=%async_computation.2 | async-start | bytes 7077888 | tf_op jit(solution)/shard_map/all_to_all | solution.py:79
  1162.4 180.6 %all-to-all-start.3 = ((bf16[8,2,110592]{2,1,0:T(2,128)(2,1)}), bf16[8,2,110592]{2,1,0:T(2,128)(2,1)}, u32[]{:S(2)}, u32[]{:S(2)}) async-start(bf16[8,2,110592]{2,1,0:T(2,128)(2,1)} %reshape.235), calls=%async_computation.5 | async-start | bytes 7077888 | tf_op jit(solution)/shard_map/all_to_all | solution.py:79
  1392.7 11.1 copy-start.1
Sparse Core Ops, SparseCore 0:
  163.8 243.9 all-gather.2
  409.3 242.0 all-gather.4
  653.8 235.3 reduce-scatter.5
  891.5 238.2 reduce-scatter.7
  1133.2 139.5 reduce-scatter.9
where the time goes:
time: 1420 us; the launch traced here: 1410 us
  waiting for transfers between devices  628 us (44%)
  local copies, waits for them, and re-layouts  496 us (35%)
  matrix products  130 us (9%)
  blocking collectives  93.8 us (7%)
  other arithmetic  39.6 us (3%)
    reduce_scatter x2, waiting for transfers between devices, legendre_inverse(): lax.psum_scatter(terms.astype(jnp.bfloat16), 'lon', scatter_dimension=2,...  264 us
    all_gather x2, waiting for transfers between devices, legendre_forward(): lax.all_gather(waves, 'lon', axis=2, tiled=True)  259 us
    unnamed x20, local copies, waits for them, and re-layouts  176 us
    unnamed x6, waiting for transfers between devices  106 us
    all_to_all x2, blocking collectives, to_waves(): lax.all_to_all(local_waves, 'lat', split_axis=0, concat_axis=3, tiled=True)  93.8 us
    all_to_all x4, local copies, waits for them, and re-layouts, to_waves(): lax.all_to_all(local_waves, 'lat', split_axis=0, concat_axis=3, tiled=True)  63.2 us
    all_to_all x2, local copies, waits for them, and re-layouts, to_grid(): lax.all_to_all(waves, 'lat', split_axis=3, concat_axis=0, tiled=True)  44 us
    convert_element_type x2, local copies, waits for them, and re-layouts, legendre_inverse(): terms.astype(jnp.bfloat16)  34.4 us
  transfers between devices with their start and end apart: 7, of which 5 were waited for; matrix products, arithmetic and copies ran while one was open for 34% of the time, Pallas kernels for 0%

commit v1 on v0

v1 whole, which is shorter than its diff:
```python
import math

import jax
import jax.numpy as jnp
import numpy as np
from jax import lax
from jax.experimental import pallas as pl
from jax.experimental.pallas import tpu as pltpu
from jax.sharding import PartitionSpec as P


CHUNKS = 2


def wave_table(longitudes, wavenumbers):
    wave_index = np.arange(wavenumbers, dtype=np.int64)[:, None]
    column = np.arange(longitudes, dtype=np.int64)[None, :]
    phase = (column * wave_index % longitudes).astype(np.float32) * np.float32(
        2.0 * math.pi / longitudes
    )
    factor = np.float32(1.0 / math.sqrt(longitudes))
    table = np.stack([np.cos(phase) * factor, -np.sin(phase) * factor], axis=1)
    return table.reshape(2 * wavenumbers, longitudes).astype(jnp.bfloat16)


def swap(blocks, axis):
    return lax.all_to_all(blocks, axis, split_axis=0, concat_axis=0)


def group_of(count, most):
    return max(size for size in range(1, most + 1) if count % size == 0)


def limits(flops, moved):
    return dict(
        compiler_params=pltpu.CompilerParams(vmem_limit_bytes=40 * 1024 * 1024),
        cost_estimate=pl.CostEstimate(flops=flops, bytes_accessed=moved, transcendentals=0),
    )


def lanes(pieces):
    return jnp.concatenate(pieces, axis=1)


def tiles(count):
    return -(-count // 128)


def put(wide, where, value):
    count = value.shape[1]
    spare = 128 * wide.shape[0] - count
    if spare:
        value = lanes([value, jnp.zeros((value.shape[0], spare), value.dtype)])
    for t in range(wide.shape[0]):
        wide[t, where, :] = value[:, 128 * t : 128 * (t + 1)]


def take(wide, where, count):
    return lanes([wide[t, where, :] for t in range(wide.shape[0])])[:, :count]


def gather_rows_kernel(chan, got_ref, out_ref, wide):
    lats, count, _ = got_ref.shape
    rows = got_ref.shape[2] // chan
    loaded = [got_ref[p].astype(jnp.float32) for p in range(lats)]
    for c in range(chan):
        piece = lanes([part[:, c * rows : (c + 1) * rows] for part in loaded])
        put(wide, pl.ds(c, count, stride=chan), piece)
    for m in range(out_ref.shape[0]):
        own = pl.ds(2 * chan * m, 2 * chan)
        out_ref[m] = take(wide, own, out_ref.shape[2]).astype(out_ref.dtype)


def gather_rows(got, chan):
    lats, count, flat = got.shape
    rows = flat // chan
    waves = count // 2
    step_waves = 8 if waves % 8 == 0 else waves
    return pl.pallas_call(
        lambda *refs: gather_rows_kernel(chan, *refs),
        grid=(waves // step_waves,),
        in_specs=[pl.BlockSpec((lats, 2 * step_waves, flat), lambda step: (0, step, 0))],
        out_specs=pl.BlockSpec((step_waves, 2 * chan, lats * rows), lambda step: (step, 0, 0)),
        out_shape=jax.ShapeDtypeStruct((waves, 2 * chan, lats * rows), got.dtype),
        scratch_shapes=[pltpu.VMEM((tiles(lats * rows), 2 * step_waves * chan, 128), jnp.float32)],
        **limits(0, 4 * got.size),
    )(got)


def analyse_kernel(table_ref, waves_ref, out_ref):
    results = [
        lax.dot_general(
            table_ref[m], waves_ref[m], (((1,), (1,)), ((), ())), preferred_element_type=jnp.float32
        )
        for m in range(table_ref.shape[0])
    ]
    out_ref[...] = lanes(results).astype(out_ref.dtype).reshape(out_ref.shape)


def analyse(table, waves, lons, first):
    width, degrees, latitudes = table.shape
    parts = waves.shape[1]
    group = math.lcm(parts, 128) // parts
    group = group if width % group == 0 else width
    offset = first // group
    out = jax.ShapeDtypeStruct((lons, degrees // lons, width * parts), waves.dtype)
    return pl.pallas_call(
        analyse_kernel,
        grid=(width // group,),
        in_specs=[
            pl.BlockSpec((group, degrees, latitudes), lambda step: (step, 0, 0)),
            pl.BlockSpec((group, parts, latitudes), lambda step: (step + offset, 0, 0)),
        ],
        out_specs=pl.BlockSpec((lons, degrees // lons, group * parts), lambda step: (0, 0, step)),
        out_shape=out,
        **limits(
            2 * width * degrees * latitudes * parts,
            2 * width * (degrees * latitudes + (degrees + latitudes) * parts),
        ),
    )(table, waves)


def synthesise_kernel(chan, table_ref, got_ref, out_ref, wide):
    group = table_ref.shape[0]
    degrees = table_ref.shape[1]
    lats = out_ref.shape[0]
    latitudes = table_ref.shape[2]
    rows = latitudes // lats
    parts = 2 * chan
    mixed = got_ref[...].reshape(degrees, group * parts).astype(jnp.float32)
    for m in range(group):
        one = mixed[:, m * parts : (m + 1) * parts].astype(table_ref.dtype)
        back = lax.dot_general(
            one, table_ref[m], (((0,), (0,)), ((), ())), preferred_element_type=jnp.float32
        )
        put(wide, pl.ds(m * parts, parts), back)
    per = math.lcm(rows, 128) // rows
    per = per if chan % per == 0 else chan
    for c in range(0, chan, per):
        taken = [
            take(wide, pl.ds(c + i, 2 * group, stride=chan), latitudes) for i in range(per)
        ]
        for p in range(lats):
            piece = lanes([one[:, p * rows : (p + 1) * rows] for one in taken])
            out_ref[p, :, c * rows : (c + per) * rows] = piece.astype(out_ref.dtype)


def synthesise(table, got, lats, chan):
    width, degrees, latitudes = table.shape
    lons, degrees_here, flat = got.shape
    parts = 2 * chan
    group = 8 if width % 8 == 0 else width
    return pl.pallas_call(
        lambda *refs: synthesise_kernel(chan, *refs),
        grid=(width // group,),
        in_specs=[
            pl.BlockSpec((group, degrees, latitudes), lambda step: (step, 0, 0)),
            pl.BlockSpec((lons, degrees_here, group * parts), lambda step: (0, 0, step)),
        ],
        out_specs=pl.BlockSpec(
            (lats, 2 * group, chan * latitudes // lats), lambda step: (0, step, 0)
        ),
        out_shape=jax.ShapeDtypeStruct((lats, 2 * width, chan * latitudes // lats), got.dtype),
        scratch_shapes=[pltpu.VMEM((tiles(latitudes), group * parts, 128), jnp.float32)],
        **limits(
            2 * width * degrees * latitudes * parts,
            2 * width * (degrees * latitudes + (degrees + latitudes) * parts),
        ),
    )(table, got)


def mix_kernel(adjoint, got_ref, weight_ref, sent_ref, spec_ref, wide):
    sign = -1.0 if adjoint else 1.0
    inner = 0 if adjoint else 1
    lons, group, flat = got_ref.shape
    rows, total_chan = spec_ref.shape[1:]
    width = rows // 2
    chan = total_chan // lons
    loaded = [got_ref[q].astype(jnp.float32) for q in range(lons)]
    for m in range(width):
        for k in range(2):
            lower = (2 * m + k) * chan
            piece = lanes([part[:, lower : lower + chan] for part in loaded])
            put(wide, pl.ds(k * width + m, group, stride=rows), piece)
    for index in range(group):
        own = pl.ds(index * rows, rows)
        both = take(wide, own, total_chan).astype(spec_ref.dtype)
        spec_ref[index] = both
        by_real, by_imag = (
            lax.dot_general(
                both,
                weight_ref[index, part],
                (((1,), (inner,)), ((), ())),
                preferred_element_type=jnp.float32,
            )
            for part in range(2)
        )
        real_out = by_real[:width] - sign * by_imag[width:]
        imag_out = by_real[width:] + sign * by_imag[:width]
        put(wide, own, jnp.concatenate([real_out, imag_out], axis=0))
    per = math.lcm(2 * chan, 128) // (2 * chan)
    per = per if width % per == 0 else width
    for m in range(0, width, per):
        taken = [
            take(wide, pl.ds(k * width + m + i, group, stride=rows), total_chan)
            for i in range(per)
            for k in range(2)
        ]
        for q in range(lons):
            piece = lanes([one[:, q * chan : (q + 1) * chan] for one in taken])
            lower = 2 * m * chan
            sent_ref[q, :, lower : lower + 2 * per * chan] = piece.astype(sent_ref.dtype)


def mix(got, weight, adjoint):
    lons, degrees, flat = got.shape
    total_chan = weight.shape[2]
    rows = flat * lons // total_chan
    group = 16 if degrees % 16 == 0 else degrees
    return pl.pallas_call(
        lambda *refs: mix_kernel(adjoint, *refs),
        grid=(degrees // group,),
        in_specs=[
            pl.BlockSpec((lons, group, flat), lambda step: (0, step, 0)),
            pl.BlockSpec((group, 2, total_chan, total_chan), lambda step: (step, 0, 0, 0)),
        ],
        out_specs=[
            pl.BlockSpec((lons, group, flat), lambda step: (0, step, 0)),
            pl.BlockSpec((group, rows, total_chan), lambda step: (step, 0, 0)),
        ],
        out_shape=[
            jax.ShapeDtypeStruct(got.shape, got.dtype),
            jax.ShapeDtypeStruct((degrees, rows, total_chan), got.dtype),
        ],
        scratch_shapes=[pltpu.VMEM((tiles(total_chan), group * rows, 128), jnp.float32)],
        **limits(4 * degrees * rows * total_chan**2, 2 * (weight.size + 3 * got.size)),
    )(got, weight)


def term_kernel(chunks, *refs):
    out_ref = refs[-1]
    chan = out_ref.shape[0]

    def over_rows(left, right):
        return lax.dot_general(
            left, right, (((0,), (0,)), ((), ())), preferred_element_type=jnp.float32
        )

    for index in range(refs[0].shape[0]):
        real_term = jnp.zeros((chan, chan), jnp.float32)
        imag_term = jnp.zeros((chan, chan), jnp.float32)
        for chunk in range(chunks):
            spec = refs[chunk][index]
            grad = refs[chunks + chunk][index]
            half = spec.shape[0] // 2
            wide = spec.astype(jnp.float32)
            turned = jnp.concatenate([-wide[half:], wide[:half]], axis=0).astype(spec.dtype)
            real_term += over_rows(grad, spec)
            imag_term += over_rows(grad, turned)
        both = jnp.concatenate([real_term, imag_term], axis=1)
        out_ref[:, 2 * chan * index : 2 * chan * (index + 1)] = both.astype(out_ref.dtype)


def weight_terms(specs, grads):
    degrees, rows, chan = specs[0].shape
    chunks = len(specs)
    group = group_of(degrees, 8)
    return pl.pallas_call(
        lambda *refs: term_kernel(chunks, *refs),
        grid=(degrees // group,),
        in_specs=[pl.BlockSpec((group, rows, chan), lambda step: (step, 0, 0))] * (2 * chunks),
        out_specs=pl.BlockSpec((chan, group * 2 * chan), lambda step: (0, step)),
        out_shape=jax.ShapeDtypeStruct((chan, degrees * 2 * chan), specs[0].dtype),
        compiler_params=pltpu.CompilerParams(vmem_limit_bytes=32 * 1024 * 1024),
        cost_estimate=pl.CostEstimate(
            flops=4 * chunks * degrees * rows * chan * chan,
            bytes_accessed=4 * degrees * chan * (chunks * rows + chan),
            transcendentals=0,
        ),
    )(*specs, *grads)


def on_device(field, cotangent, legendre, spectral_weight):
    lats = lax.axis_size("lat")
    lons = lax.axis_size("lon")
    chan, rows, longitudes = field.shape
    waves_here, degrees_here, latitudes = legendre.shape
    total_chan = chan * lons
    degrees = degrees_here * lons
    total_waves = waves_here * lats
    chunks = CHUNKS if waves_here % (8 * CHUNKS) == 0 else 1
    width = waves_here // chunks
    fourier = jnp.asarray(wave_table(longitudes, total_waves))
    f32 = jnp.float32
    bf16 = jnp.bfloat16

    tables = [
        lax.all_gather(legendre[j * width : (j + 1) * width], "lon", axis=1, tiled=True)
        for j in range(chunks)
    ]

    def to_waves(grid):
        flat = grid.reshape(chan * rows, longitudes)
        local = lax.dot_general(fourier, flat, (((1,), (1,)), ((), ())), preferred_element_type=f32)
        local = local.astype(bf16).reshape(lats, waves_here * 2, chan * rows)
        return gather_rows(swap(local, "lat"), chan)

    def to_grid(parts):
        got = jnp.concatenate(parts, axis=1)
        return lax.dot_general(
            got.reshape(total_waves * 2, chan * rows),
            fourier,
            (((0,), (0,)), ((), ())),
            preferred_element_type=f32,
        ).reshape(chan, rows, longitudes)

    def finish(mixed, table):
        return swap(synthesise(table, swap(mixed, "lon"), lats, chan), "lat")

    waves = to_waves(field)
    grad_waves = to_waves(cotangent)
    specs, grads, backs, grad_backs = [], [], [], []
    ready = None
    for j in range(chunks):
        table = tables[j]
        if ready is None:
            table, waves, grad_waves = lax.optimization_barrier((table, waves, grad_waves))
        else:
            table, mixed, grad_mixed = lax.optimization_barrier((table, *ready))
        got = swap(analyse(table, waves, lons, j * width), "lon")
        grad_got = swap(analyse(table, grad_waves, lons, j * width), "lon")
        if ready is not None:
            backs.append(finish(mixed, tables[j - 1]))
            grad_backs.append(finish(grad_mixed, tables[j - 1]))
        mixed, spec = mix(got, spectral_weight, False)
        grad_mixed, grad = mix(grad_got, spectral_weight, True)
        specs.append(spec)
        grads.append(grad)
        ready = (mixed, grad_mixed)
    backs.append(finish(mixed, table))
    grad_backs.append(finish(grad_mixed, table))
    terms = weight_terms(specs, grads)
    summed = lax.psum_scatter(terms, "lat", scatter_dimension=0, tiled=True)
    weight_grad = summed.reshape(-1, degrees_here, 2, total_chan).transpose(1, 2, 0, 3)
    output = (field.astype(f32) + to_grid(backs)).astype(bf16)
    field_grad = (cotangent.astype(f32) + to_grid(grad_backs)).astype(bf16)
    return (output, field_grad, weight_grad)


def solution(mesh):
    placed = (
        P("lon", "lat", None),
        P("lon", "lat", None),
        P("lat", "lon", None),
        P("lon", None, None, None),
    )
    return jax.shard_map(
        on_device,
        mesh=mesh,
        in_specs=placed,
        out_specs=(P("lon", "lat", None), P("lon", "lat", None), P("lon", None, "lat", None)),
        check_vma=False,
    )
```

time: 1420 us -> 805 us (0.57)
  local copies, waits for them, and re-layouts: 496 us -> 67.8 us
  waiting for transfers between devices: 628 us -> 402 us
  Pallas kernels: 0 us -> 111 us
  matrix products: 130 us -> 41.9 us
  starting transfers between devices: 8.73 us -> 46.7 us
  other arithmetic: 39.6 us -> 4.48 us
  blocking collectives: 93.8 us -> 115 us
    all_to_all x2 -> x11, waiting for transfers between devices: 0.01 us -> 385 us  [swap(): return lax.all_to_all(blocks, axis, split_axis=0, concat_axis=0)]
    reduce_scatter x2 -> x1, waiting for transfers between devices: 264 us -> 0.01 us  [on_device(): summed = lax.psum_scatter(terms, 'lat', scatter_dimension=0, tiled=True)]
    all_gather x2, waiting for transfers between devices: 259 us -> 16.9 us  [on_device(): lax.all_gather(legendre[j * width:(j + 1) * width], 'lon', axis=1, tiled=...]
    unnamed x20 -> x66, local copies, waits for them, and re-layouts: 176 us -> 48.4 us
    pallas_call x0 -> x15, Pallas kernels: none -> 111 us  [the longest x4 49.1 us: mix(): pl.pallas_call(lambda *refs: mix_kernel(adjoint, *refs), grid=(degrees //...]
    all_to_all x6 -> x0, local copies, waits for them, and re-layouts: 107 us -> none  [the longest x4 63.2 us: to_waves(): lax.all_to_all(local_waves, 'lat', split_axis=0, concat_axis=3, tiled=True)]
    unnamed x6 -> x3, waiting for transfers between devices: 106 us -> 0.73 us
    dot_general x11 -> x4, matrix products: 130 us -> 41.9 us  [the longest x2 21 us: to_waves(): lax.dot_general(fourier, flat, (((1,), (1,)), ((), ())), preferred_elemen...]
  transfers between devices with their start and end apart: 7 -> 14, of which waited for: 5 -> 12; matrix products, arithmetic and copies ran while one was open for 34% -> 7% of each run, Pallas kernels for 0% -> 10%
where the time goes in v1:
time: 805 us; the launch traced here: 803 us
  waiting for transfers between devices  402 us (50%)
  blocking collectives  115 us (14%)
  Pallas kernels  111 us (14%)
  local copies, waits for them, and re-layouts  67.8 us (8%)
  starting transfers between devices  46.7 us (6%)
  matrix products  41.9 us (5%)
  between operations  14.1 us (2%)
    all_to_all x11, waiting for transfers between devices, swap(): return lax.all_to_all(blocks, axis, split_axis=0, concat_axis=0)  385 us
    all_to_all x3, blocking collectives, swap(): return lax.all_to_all(blocks, axis, split_axis=0, concat_axis=0)  115 us
    pallas_call x4, Pallas kernels, mix(): pl.pallas_call(lambda *refs: mix_kernel(adjoint, *refs), grid=(degrees //...  49.1 us
    unnamed x66, local copies, waits for them, and re-layouts  48.4 us
    all_to_all x11, starting transfers between devices, swap(): return lax.all_to_all(blocks, axis, split_axis=0, concat_axis=0)  46.5 us
    pallas_call x4, Pallas kernels, synthesise(): pl.pallas_call(lambda *refs: synthesise_kernel(chan, *refs), grid=(width...  23.2 us
    dot_general x2, matrix products, to_waves(): lax.dot_general(fourier, flat, (((1,), (1,)), ((), ())), preferred_elemen...  21 us
    dot_general x2, matrix products, to_grid(): lax.dot_general(got.reshape(total_waves * 2, chan * rows), fourier, (((0,...  20.9 us
  transfers between devices with their start and end apart: 14, of which 12 were waited for; matrix products, arithmetic and copies ran while one was open for 7% of the time, Pallas kernels for 10%

profile of v1, /device:TPU:0, one launch (start us, length us, event | category | flops | bytes accessed | tf_op | source)
XLA Modules:
  0.0 803.1 jit_solution(3445387334081047353)
XLA Ops:
  7.2 4.4 fusion
  11.6 10.4 %convolution_convert_fusion = bf16[768,2304]{1,0:T(8,128)(2,1)} fusion(bf16[768,1440]{0,1:T(8,128)(2,1)S(1)} %copy-done.32, bf16[2304,1440]{1,0:T(8,128)(2,1)} %bitcast.32), kind=kOutput, calls=%fused_computation.2 | convolution fusion | flops 5097848832 | bytes 12386304 | tf_op jit(solution)/shard_map/dot_general | solution.py:304
  22.0 5.2 all-to-all-start.1
  27.9 10.6 %convolution_convert_fusion.1 = bf16[768,2304]{1,0:T(8,128)(2,1)} fusion(bf16[768,1440]{0,1:T(8,128)(2,1)} %constant.2.clone, bf16[2304,1440]{1,0:T(8,128)(2,1)} %bitcast.31), kind=kOutput, calls=%fused_computation.3 | convolution fusion | flops 5097848832 | bytes 12386304 | tf_op jit(solution)/shard_map/dot_general | solution.py:304
  38.5 30.7 %all-to-all-done.1.refs_0_ = bf16[8,96,2304]{2,1,0:T(8,128)(2,1)S(1)} async-done(((bf16[8,96,2304]{2,1,0:T(8,128)(2,1)}), bf16[8,96,2304]{2,1,0:T(8,128)(2,1)S(1)}, u32[]{:S(2)}, u32[]{:S(2)}) %all-to-all-start.1) | async-done | bytes 3538976 | tf_op jit(solution)/shard_map/all_to_all | solution.py:27
  69.2 1.8 copy-done.11
  71.0 4.5 all-to-all-start
  75.5 2.0 copy-done.12
  77.5 4.8 shard_map.77.waves_ref
  82.3 35.3 %all-to-all-done.refs_0_ = bf16[8,96,2304]{2,1,0:T(8,128)(2,1)} async-done(((bf16[8,96,2304]{2,1,0:T(8,128)(2,1)}), bf16[8,96,2304]{2,1,0:T(8,128)(2,1)}, u32[]{:S(2)}, u32[]{:S(2)}) %all-to-all-start) | async-done | bytes 3538976 | tf_op jit(solution)/shard_map/all_to_all | solution.py:27
  117.6 6.3 shard_map.76.waves_ref
  124.0 1.8 copy-done.8
  125.7 16.9 %all-gather.3.cloned.1.call-done.table_ref.refs_0_ = bf16[24,384,384]{2,1,0:T(8,128)(2,1)} async-done(((bf16[24,96,384]{2,1,0:T(8,128)(2,1)}), bf16[24,384,384]{2,1,0:T(8,128)(2,1)}) %all-gather.3.cloned.1.call-update) | async-done | bytes 7077904 | tf_op jit(solution)/shard_map/all_gather | solution.py:298
  142.7 3.0 copy-done.4
  145.7 2.0 copy-done.9
  147.7 3.4 shard_map.78
  152.3 4.4 all-to-all-start.2
  156.7 3.0 copy-done.5
  159.7 3.4 shard_map.80
  164.3 82.3 %all-to-all-done.2.refs_0_ = bf16[4,96,2304]{2,1,0:T(8,128)(2,1)} async-done(((bf16[4,96,2304]{2,1,0:T(8,128)(2,1)}), bf16[4,96,2304]{2,1,0:T(8,128)(2,1)}, u32[]{:S(2)}, u32[]{:S(2)}) %all-to-all-start.2) | async-done | bytes 1769504 | tf_op jit(solution)/shard_map/all_to_all | solution.py:27
  246.6 4.6 all-to-all-start.3
  251.2 12.5 %shard_map.79 = (bf16[4,96,2304]{2,1,0:T(8,128)(2,1)S(1)}, bf16[96,48,192]{2,1,0:T(8,128)(2,1)S(1)}) custom-call(bf16[4,96,2304]{2,1,0:T(8,128)(2,1)} %all-to-all-done.2.refs_0_, bf16[96,2,192,192]{3,2,1,0:T(8,128)(2,1)} %refs_1_.7), custom_call_target="tpu_custom_call" | custom-call | flops 679477248 | bytes 19464192 | tf_op jit(solution)/shard_map/pallas_call | solution.py:220
  266.4 65.4 %all-to-all-done.3.refs_0_ = bf16[4,96,2304]{2,1,0:T(8,128)(2,1)} async-done(((bf16[4,96,2304]{2,1,0:T(8,128)(2,1)}), bf16[4,96,2304]{2,1,0:T(8,128)(2,1)}, u32[]{:S(2)}, u32[]{:S(2)}) %all-to-all-start.3) | async-done | bytes 1769504 | tf_op jit(solution)/shard_map/all_to_all | solution.py:27
  331.8 12.1 %shard_map.81 = (bf16[4,96,2304]{2,1,0:T(8,128)(2,1)S(1)}, bf16[96,48,192]{2,1,0:T(8,128)(2,1)S(1)}) custom-call(bf16[4,96,2304]{2,1,0:T(8,128)(2,1)} %all-to-all-done.3.refs_0_, bf16[96,2,192,192]{3,2,1,0:T(8,128)(2,1)} %refs_1_.7), custom_call_target="tpu_custom_call" | custom-call | flops 679477248 | bytes 19464192 | tf_op jit(solution)/shard_map/pallas_call | solution.py:220
  346.5 3.0 copy-done
  349.5 3.3 shard_map.87
  354.0 4.7 all-to-all-start.11
  358.7 3.0 copy-done.1
  361.7 3.3 shard_map.83
  366.3 34.2 %all-to-all-done.11.refs_0_ = bf16[4,96,2304]{2,1,0:T(8,128)(2,1)} async-done(((bf16[4,96,2304]{2,1,0:T(8,128)(2,1)}), bf16[4,96,2304]{2,1,0:T(8,128)(2,1)}, u32[]{:S(2)}, u32[]{:S(2)}) %all-to-all-start.11) | async-done | bytes 1769504 | tf_op jit(solution)/shard_map/all_to_all | solution.py:27
  400.5 3.6 all-to-all-start.6
  404.1 12.1 %shard_map.88 = (bf16[4,96,2304]{2,1,0:T(8,128)(2,1)S(1)}, bf16[96,48,192]{2,1,0:T(8,128)(2,1)S(1)}) custom-call(bf16[4,96,2304]{2,1,0:T(8,128)(2,1)} %all-to-all-done.11.refs_0_, bf16[96,2,192,192]{3,2,1,0:T(8,128)(2,1)} %refs_1_.7), custom_call_target="tpu_custom_call" | custom-call | flops 679477248 | bytes 19464192 | tf_op jit(solution)/shard_map/pallas_call | solution.py:220
  418.8 26.1 %all-to-all-done.6.refs_0_ = bf16[4,96,2304]{2,1,0:T(8,128)(2,1)S(1)} async-done(((bf16[4,96,2304]{2,1,0:T(8,128)(2,1)}), bf16[4,96,2304]{2,1,0:T(8,128)(2,1)S(1)}, u32[]{:S(2)}, u32[]{:S(2)}) %all-to-all-start.6) | async-done | bytes 1769504 | tf_op jit(solution)/shard_map/all_to_all | solution.py:27
  444.9 12.5 %shard_map.84 = (bf16[4,96,2304]{2,1,0:T(8,128)(2,1)S(1)}, bf16[96,48,192]{2,1,0:T(8,128)(2,1)S(1)}) custom-call(bf16[4,96,2304]{2,1,0:T(8,128)(2,1)S(1)} %all-to-all-done.6.refs_0_, bf16[96,2,192,192]{3,2,1,0:T(8,128)(2,1)} %refs_1_.7), custom_call_target="tpu_custom_call" | custom-call | flops 679477248 | bytes 19464192 | tf_op jit(solution)/shard_map/pallas_call | solution.py:220
  458.7 14.5 %shard_map.90 = bf16[192,36864]{1,0:T(8,128)(2,1)} custom-call(bf16[96,48,192]{2,1,0:T(8,128)(2,1)S(1)} %copy-done.18, bf16[96,48,192]{2,1,0:T(8,128)(2,1)S(1)} %get-tuple-element.28.refs_1_, bf16[96,48,192]{2,1,0:T(8,128)(2,1)S(1)} %copy-done.20, bf16[96,48,192]{2,1,0:T(8,128)(2,1)S(1)} %copy-done.22), custom_call_target="tpu_custom_call" | custom-call | flops 1358954496 | bytes 21233664 | tf_op jit(solution)/shard_map/pallas_call | solution.py:268
  474.7 43.2 %all_to_all.70.refs_1_ = bf16[4,96,2304]{2,1,0:T(8,128)(2,1)S(1)} all-to-all(bf16[4,96,2304]{2,1,0:T(8,128)(2,1)S(1)} %copy-done.24), channel_id=1, replica_groups=mesh['lat'=8,'lon'=4] {'lon'}, dimensions={0} | all-to-all | bytes 3538944 | tf_op jit(solution)/shard_map/all_to_all | solution.py:27
  517.8 3.6 all-to-all-start.9
  521.4 3.0 copy-done.6
  524.5 6.0 shard_map.82
  530.4 31.3 %all-to-all-done.9.refs_1_ = bf16[4,96,2304]{2,1,0:T(8,128)(2,1)S(1)} async-done(((bf16[4,96,2304]{2,1,0:T(8,128)(2,1)}), bf16[4,96,2304]{2,1,0:T(8,128)(2,1)S(1)}, u32[]{:S(2)}, u32[]{:S(2)}) %all-to-all-start.9) | async-done | bytes 1769504 | tf_op jit(solution)/shard_map/all_to_all | solution.py:27
  561.8 4.3 all-to-all-start.5
  566.1 3.1 copy-done.7
  569.3 5.2 shard_map.86
  574.5 16.6 %all-to-all-done.5 = bf16[8,48,2304]{2,1,0:T(8,128)(2,1)} async-done(((bf16[8,48,2304]{2,1,0:T(8,128)(2,1)}), bf16[8,48,2304]{2,1,0:T(8,128)(2,1)}, u32[]{:S(2)}, u32[]{:S(2)}) %all-to-all-start.5) | async-done | bytes 1769504 | tf_op jit(solution)/shard_map/all_to_all | solution.py:27
  591.2 26.2 %all_to_all.71 = bf16[8,48,2304]{2,1,0:T(8,128)(2,1)} all-to-all(bf16[8,48,2304]{2,1,0:T(8,128)(2,1)S(1)} %shard_map.86), channel_id=1, replica_groups=mesh['lat'=8,'lon'=4] {'lat'}, dimensions={0} | all-to-all | bytes 3538944 | tf_op jit(solution)/shard_map/all_to_all | solution.py:27
  617.4 45.3 %all_to_all.72.refs_1_ = bf16[4,96,2304]{2,1,0:T(8,128)(2,1)S(1)} all-to-all(bf16[4,96,2304]{2,1,0:T(8,128)(2,1)S(1)} %copy-done.27), channel_id=1, replica_groups=mesh['lat'=8,'lon'=4] {'lon'}, dimensions={0} | all-to-all | bytes 3538944 | tf_op jit(solution)/shard_map/all_to_all | solution.py:27
  662.6 3.8 all-to-all-start.7
  666.5 3.0 copy-done.2
  669.5 6.0 shard_map.89
  675.4 31.2 %all-to-all-done.7.refs_1_ = bf16[4,96,2304]{2,1,0:T(8,128)(2,1)S(1)} async-done(((bf16[4,96,2304]{2,1,0:T(8,128)(2,1)}), bf16[4,96,2304]{2,1,0:T(8,128)(2,1)S(1)}, u32[]{:S(2)}, u32[]{:S(2)}) %all-to-all-start.7) | async-done | bytes 1769504 | tf_op jit(solution)/shard_map/all_to_all | solution.py:27
  706.6 3.6 all-to-all-start.13
  710.2 3.0 copy-done.3
  713.2 6.0 shard_map.85
  719.2 14.1 %all-to-all-done.13 = bf16[8,48,2304]{2,1,0:T(8,128)(2,1)S(1)} async-done(((bf16[8,48,2304]{2,1,0:T(8,128)(2,1)}), bf16[8,48,2304]{2,1,0:T(8,128)(2,1)S(1)}, u32[]{:S(2)}, u32[]{:S(2)}) %all-to-all-start.13) | async-done | bytes 1769504 | tf_op jit(solution)/shard_map/all_to_all | solution.py:27
  734.5 4.3 all-to-all-start.8
  738.8 2.2 pad_maximum_fusion.1
  741.0 3.6 copy.9
  744.7 17.3 %all-to-all-done.8 = bf16[8,48,2304]{2,1,0:T(8,128)(2,1)} async-done(((bf16[8,48,2304]{2,1,0:T(8,128)(2,1)}), bf16[8,48,2304]{2,1,0:T(8,128)(2,1)}, u32[]{:S(2)}, u32[]{:S(2)}) %all-to-all-start.8) | async-done | bytes 1769504 | tf_op jit(solution)/shard_map/all_to_all | solution.py:27
  761.9 2.2 pad_maximum_fusion
  764.2 3.6 copy.8
  767.7 11.1 %add_convert_fusion.1 = bf16[48,48,1440]{2,1,0:T(8,128)(2,1)} fusion(bf16[48,48,1440]{2,1,0:T(8,128)(2,1)} %param.5, bf16[48,48,768]{2,1,0:T(8,128)(2,1)} %bitcast.29, bf16[768,1440,1]{0,1,2:T(8,128)(2,1)} %constant.3), kind=kOutput, calls=%fused_computation.1 | convolution fusion | flops 5106032640 | bytes 19021824 | tf_op jit(solution)/shard_map/dot_general | solution.py:310
  778.8 9.9 %add_convert_fusion = bf16[48,48,1440]{2,1,0:T(8,128)(2,1)} fusion(bf16[48,48,1440]{2,1,0:T(8,128)(2,1)} %param.6, bf16[48,48,768]{2,1,0:T(8,128)(2,1)S(1)} %bitcast.27, bf16[768,1440,1]{0,1,2:T(8,128)(2,1)S(1)} %copy-done.31), kind=kOutput, calls=%fused_computation | convolution fusion | flops 5106032640 | bytes 19021824 | tf_op jit(solution)/shard_map/dot_general | solution.py:310
  788.7 3.9 reshape.37
  792.6 3.9 copy.12
  (62 shorter events, 17.5 us)
Async XLA Ops:
  7.2 4.4 copy-start.32
  7.2 135.5 %all-gather.3.cloned.1.call-start = ((), (), s32[]{:S(2)}) async-start(), calls=%async_computation.15 | async-start | bytes 8847360 | tf_op jit(solution)/shard_map/all_gather | solution.py:298
  22.0 47.3 %all-to-all-start.1 = ((bf16[8,96,2304]{2,1,0:T(8,128)(2,1)}), bf16[8,96,2304]{2,1,0:T(8,128)(2,1)S(1)}, u32[]{:S(2)}, u32[]{:S(2)}) async-start(bf16[8,96,2304]{2,1,0:T(8,128)(2,1)} %bitcast.26), calls=%async_computation.1 | async-start | bytes 7077888 | tf_op jit(solution)/shard_map/all_to_all | solution.py:27
  27.1 319.3 %all-gather.5.cloned.1.call-start = ((), (), s32[]{:S(2)}) async-start(), calls=%async_computation.16 | async-start | bytes 8847360 | tf_op jit(solution)/shard_map/all_gather | solution.py:298
  69.2 1.8 copy-start.11
  71.0 46.6 %all-to-all-start = ((bf16[8,96,2304]{2,1,0:T(8,128)(2,1)}), bf16[8,96,2304]{2,1,0:T(8,128)(2,1)}, u32[]{:S(2)}, u32[]{:S(2)}) async-start(bf16[8,96,2304]{2,1,0:T(8,128)(2,1)} %bitcast.28), calls=%async_computation | async-start | bytes 7077888 | tf_op jit(solution)/shard_map/all_to_all | solution.py:27
  75.5 2.0 copy-start.12
  123.9 1.8 copy-start.8
  142.7 3.0 copy-start.4
  145.7 2.0 copy-start.9
  151.0 1.2 copy-start.16
  152.3 94.4 %all-to-all-start.2 = ((bf16[4,96,2304]{2,1,0:T(8,128)(2,1)}), bf16[4,96,2304]{2,1,0:T(8,128)(2,1)}, u32[]{:S(2)}, u32[]{:S(2)}) async-start(bf16[4,96,2304]{2,1,0:T(8,128)(2,1)} %copy-done.16), calls=%async_computation.2 | async-start | bytes 3538944 | tf_op jit(solution)/shard_map/all_to_all | solution.py:27
  156.7 3.0 copy-start.5
  163.1 1.2 copy-start.14
  246.6 85.2 %all-to-all-start.3 = ((bf16[4,96,2304]{2,1,0:T(8,128)(2,1)}), bf16[4,96,2304]{2,1,0:T(8,128)(2,1)}, u32[]{:S(2)}, u32[]{:S(2)}) async-start(bf16[4,96,2304]{2,1,0:T(8,128)(2,1)} %copy-done.14), calls=%async_computation.3 | async-start | bytes 3538944 | tf_op jit(solution)/shard_map/all_to_all | solution.py:27
  263.7 1.4 copy-start.17
  265.1 1.2 copy-start.23
  343.9 1.4 copy-start.19
  345.3 1.2 copy-start.25
  346.5 3.0 copy-start
  352.8 1.2 copy-start.15
  354.0 4.7 copy-start.10
  354.0 46.5 %all-to-all-start.11 = ((bf16[4,96,2304]{2,1,0:T(8,128)(2,1)}), bf16[4,96,2304]{2,1,0:T(8,128)(2,1)}, u32[]{:S(2)}, u32[]{:S(2)}) async-start(bf16[4,96,2304]{2,1,0:T(8,128)(2,1)} %copy-done.15), calls=%async_computation.11 | async-start | bytes 3538944 | tf_op jit(solution)/shard_map/all_to_all | solution.py:27
  358.7 3.0 copy-start.1
  365.1 1.2 copy-start.13
  400.5 44.5 %all-to-all-start.6 = ((bf16[4,96,2304]{2,1,0:T(8,128)(2,1)}), bf16[4,96,2304]{2,1,0:T(8,128)(2,1)S(1)}, u32[]{:S(2)}, u32[]{:S(2)}) async-start(bf16[4,96,2304]{2,1,0:T(8,128)(2,1)} %copy-done.13), calls=%async_computation.6 | async-start | bytes 3538944 | tf_op jit(solution)/shard_map/all_to_all | solution.py:27
  404.1 384.6 %reduce-scatter.2.cloned.1.call-start = ((), (), s32[]{:S(2)}) async-start(), calls=%async_computation.17 | async-start | bytes 15925248 | tf_op jit(solution)/shard_map/reduce_scatter | solution.py:343
  416.2 1.4 copy-start.21
  417.6 1.2 copy-start.26
  444.9 13.8 %copy-start.18 = (bf16[96,48,192]{2,1,0:T(8,128)(2,1)S(1)}, bf16[96,48,192]{2,1,0:T(8,128)(2,1)}, u32[]{:S(2)}) copy-start(bf16[96,48,192]{2,1,0:T(8,128)(2,1)} %copy-done.17) | copy-start | bytes 5308420
  444.9 13.8 %copy-start.20 = (bf16[96,48,192]{2,1,0:T(8,128)(2,1)S(1)}, bf16[96,48,192]{2,1,0:T(8,128)(2,1)}, u32[]{:S(2)}) copy-start(bf16[96,48,192]{2,1,0:T(8,128)(2,1)} %copy-done.19) | copy-start | bytes 5308420
  444.9 13.8 %copy-start.22 = (bf16[96,48,192]{2,1,0:T(8,128)(2,1)S(1)}, bf16[96,48,192]{2,1,0:T(8,128)(2,1)}, u32[]{:S(2)}) copy-start(bf16[96,48,192]{2,1,0:T(8,128)(2,1)} %copy-done.21) | copy-start | bytes 5308420
  457.5 1.2 copy-start.28
  473.2 1.5 copy-start.24
  517.8 44.0 %all-to-all-start.9 = ((bf16[4,96,2304]{2,1,0:T(8,128)(2,1)}), bf16[4,96,2304]{2,1,0:T(8,128)(2,1)S(1)}, u32[]{:S(2)}, u32[]{:S(2)}) async-start(bf16[4,96,2304]{2,1,0:T(8,128)(2,1)} %copy-done.25), calls=%async_computation.9 | async-start | bytes 3538944 | tf_op jit(solution)/shard_map/all_to_all | solution.py:27
  521.4 3.1 copy-start.6
  561.8 29.4 %all-to-all-start.5 = ((bf16[8,48,2304]{2,1,0:T(8,128)(2,1)}), bf16[8,48,2304]{2,1,0:T(8,128)(2,1)}, u32[]{:S(2)}, u32[]{:S(2)}) async-start(bf16[8,48,2304]{2,1,0:T(8,128)(2,1)} %shard_map.82), calls=%async_computation.5 | async-start | bytes 3538944 | tf_op jit(solution)/shard_map/all_to_all | solution.py:27
  566.1 3.1 copy-start.7
  574.5 42.8 %copy-start.27 = (bf16[4,96,2304]{2,1,0:T(8,128)(2,1)S(1)}, bf16[4,96,2304]{2,1,0:T(8,128)(2,1)}, u32[]{:S(2)}) copy-start(bf16[4,96,2304]{2,1,0:T(8,128)(2,1)} %copy-done.26) | copy-start | bytes 5308420
  662.6 44.0 %all-to-all-start.7 = ((bf16[4,96,2304]{2,1,0:T(8,128)(2,1)}), bf16[4,96,2304]{2,1,0:T(8,128)(2,1)S(1)}, u32[]{:S(2)}, u32[]{:S(2)}) async-start(bf16[4,96,2304]{2,1,0:T(8,128)(2,1)} %copy-done.28), calls=%async_computation.7 | async-start | bytes 3538944 | tf_op jit(solution)/shard_map/all_to_all | solution.py:27
  666.4 3.0 copy-start.2
  706.6 26.7 %all-to-all-start.13 = ((bf16[8,48,2304]{2,1,0:T(8,128)(2,1)}), bf16[8,48,2304]{2,1,0:T(8,128)(2,1)S(1)}, u32[]{:S(2)}, u32[]{:S(2)}) async-start(bf16[8,48,2304]{2,1,0:T(8,128)(2,1)} %shard_map.89), calls=%async_computation.13 | async-start | bytes 3538944 | tf_op jit(solution)/shard_map/all_to_all | solution.py:27
  710.2 3.0 copy-start.3
  733.3 1.2 copy-start.29
  734.5 27.5 %all-to-all-start.8 = ((bf16[8,48,2304]{2,1,0:T(8,128)(2,1)}), bf16[8,48,2304]{2,1,0:T(8,128)(2,1)}, u32[]{:S(2)}, u32[]{:S(2)}) async-start(bf16[8,48,2304]{2,1,0:T(8,128)(2,1)} %shard_map.85), calls=%async_computation.8 | async-start | bytes 3538944 | tf_op jit(solution)/shard_map/all_to_all | solution.py:27
  767.7 11.1 %copy-start.30 = (bf16[2304,768]{1,0:T(8,128)(2,1)S(1)}, bf16[2304,768]{1,0:T(8,128)(2,1)}, u32[]{:S(2)}) copy-start(bf16[2304,768]{1,0:T(8,128)(2,1)} %copy.9) | copy-start | bytes 10616836
  767.7 11.1 %copy-start.31 = (bf16[768,1440,1]{0,1,2:T(8,128)(2,1)S(1)}, bf16[768,1440,1]{0,1,2:T(8,128)(2,1)}, u32[]{:S(2)}) copy-start(bf16[768,1440,1]{0,1,2:T(8,128)(2,1)} %constant.3) | copy-start | bytes 6635524
Sparse Core Ops, SparseCore 0:
  11.7 130.8 all-gather.2
  144.2 201.8 all-gather.4
  473.3 101.7 reduce-scatter.1

commit v2 on v1

--- a/solution.py
+++ b/solution.py
@@ -7,9 +7,6 @@
 from jax.experimental import pallas as pl
 from jax.experimental.pallas import tpu as pltpu
 from jax.sharding import PartitionSpec as P
-
-
-CHUNKS = 2
 
 
 def wave_table(longitudes, wavenumbers):
@@ -29,6 +26,69 @@
 
 def group_of(count, most):
     return max(size for size in range(1, most + 1) if count % size == 0)
+
+
+def exchange_kernel(axes, *refs):
+    count = len(axes)
+    given, taken = refs[:count], refs[count : 2 * count]
+    send_sems, recv_sems, own_sems = refs[2 * count :]
+    barrier = pltpu.get_barrier_semaphore()
+    greeted = 0
+    for axis in sorted(set(axes)):
+        size = lax.axis_size(axis)
+        me = lax.axis_index(axis)
+        for shift in range(1, size):
+            peer = lax.rem(me + shift, size)
+            pl.semaphore_signal(
+                barrier, inc=1, device_id={axis: peer}, device_id_type=pl.DeviceIdType.MESH
+            )
+        greeted += size - 1
+    pl.semaphore_wait(barrier, greeted)
+    copies = []
+    for index, axis in enumerate(axes):
+        size = lax.axis_size(axis)
+        me = lax.axis_index(axis)
+        for shift in sorted(range(1, size), key=lambda d: -min(d, size - d)):
+            peer = lax.rem(me + shift, size)
+            copy = pltpu.make_async_remote_copy(
+                src_ref=given[index].at[peer],
+                dst_ref=taken[index].at[me],
+                send_sem=send_sems.at[index, shift],
+                recv_sem=recv_sems.at[index, shift],
+                device_id={axis: peer},
+                device_id_type=pl.DeviceIdType.MESH,
+            )
+            copy.start()
+            copies.append(copy)
+        own = pltpu.make_async_copy(
+            given[index].at[me], taken[index].at[me], own_sems.at[index]
+        )
+        own.start()
+        copies.append(own)
+    for copy in copies:
+        copy.wait()
+
+
+def exchange(number, *pairs):
+    arrays = [array for array, _ in pairs]
+    axes = tuple(axis for _, axis in pairs)
+    most = max(lax.axis_size(axis) for axis in axes)
+    count = len(arrays)
+    return pl.pallas_call(
+        lambda *refs: exchange_kernel(axes, *refs),
+        in_specs=[pl.BlockSpec(memory_space=pl.ANY)] * count,
+        out_specs=[pl.BlockSpec(memory_space=pl.ANY)] * count,
+        out_shape=[jax.ShapeDtypeStruct(array.shape, array.dtype) for array in arrays],
+        scratch_shapes=[
+            pltpu.SemaphoreType.DMA((count, most)),
+            pltpu.SemaphoreType.DMA((count, most)),
+            pltpu.SemaphoreType.DMA((count,)),
+        ],
+        compiler_params=pltpu.CompilerParams(collective_id=number, has_side_effects=True),
+        cost_estimate=pl.CostEstimate(
+            flops=0, bytes_accessed=64 * sum(array.size for array in arrays), transcendentals=0
+        ),
+    )(*arrays)
 
 
 def limits(flops, moved):
@@ -288,7 +348,7 @@
     total_chan = chan * lons
     degrees = degrees_here * lons
     total_waves = waves_here * lats
-    chunks = CHUNKS if waves_here % (8 * CHUNKS) == 0 else 1
+    chunks = 2 if waves_here % 16 == 0 else 1
     width = waves_here // chunks
     fourier = jnp.asarray(wave_table(longitudes, total_waves))
     f32 = jnp.float32
@@ -314,32 +374,58 @@
             preferred_element_type=f32,
         ).reshape(chan, rows, longitudes)
 
-    def finish(mixed, table):
-        return swap(synthesise(table, swap(mixed, "lon"), lats, chan), "lat")
-
     waves = to_waves(field)
     grad_waves = to_waves(cotangent)
+    table, waves, grad_waves = lax.optimization_barrier((tables[0], waves, grad_waves))
+    hold = lax.optimization_barrier
+
+    def forward(given, j):
+        return analyse(table, given, lons, j * width)
+
+    def finish(mixed, table):
+        return synthesise(table, mixed, lats, chan)
+
     specs, grads, backs, grad_backs = [], [], [], []
-    ready = None
-    for j in range(chunks):
-        table = tables[j]
-        if ready is None:
-            table, waves, grad_waves = lax.optimization_barrier((table, waves, grad_waves))
-        else:
-            table, mixed, grad_mixed = lax.optimization_barrier((table, *ready))
-        got = swap(analyse(table, waves, lons, j * width), "lon")
-        grad_got = swap(analyse(table, grad_waves, lons, j * width), "lon")
-        if ready is not None:
-            backs.append(finish(mixed, tables[j - 1]))
-            grad_backs.append(finish(grad_mixed, tables[j - 1]))
+    if chunks == 1:
+        got, grad_got = exchange(0, (forward(waves, 0), "lon"), (forward(grad_waves, 0), "lon"))
         mixed, spec = mix(got, spectral_weight, False)
         grad_mixed, grad = mix(grad_got, spectral_weight, True)
-        specs.append(spec)
-        grads.append(grad)
-        ready = (mixed, grad_mixed)
-    backs.append(finish(mixed, table))
-    grad_backs.append(finish(grad_mixed, table))
-    terms = weight_terms(specs, grads)
+        terms = weight_terms([spec], [grad])
+        mixed, grad_mixed, terms = hold((mixed, grad_mixed, terms))
+        mixed, grad_mixed = exchange(1, (mixed, "lon"), (grad_mixed, "lon"))
+        back, grad_back = finish(mixed, table), finish(grad_mixed, table)
+        back, grad_back = exchange(2, (back, "lat"), (grad_back, "lat"))
+        backs, grad_backs = [back], [grad_back]
+    else:
+        got, grad_got = exchange(0, (forward(waves, 0), "lon"), (forward(grad_waves, 0), "lon"))
+        mixed, spec = mix(got, spectral_weight, False)
+        grad_mixed, grad = mix(grad_got, spectral_weight, True)
+        early = table
+        table, mixed, grad_mixed = hold((tables[1], mixed, grad_mixed))
+        late_got, late_grad_got = exchange(
+            1, (forward(waves, 1), "lon"), (forward(grad_waves, 1), "lon")
+        )
+        mixed, grad_mixed, late_got, late_grad_got = hold(
+            (mixed, grad_mixed, late_got, late_grad_got)
+        )
+        mixed = swap(mixed, "lon")
+        late_mixed, late_spec = mix(late_got, spectral_weight, False)
+        late_grad_mixed, late_grad = mix(late_grad_got, spectral_weight, True)
+        terms = weight_terms([spec, late_spec], [grad, late_grad])
+        mixed, grad_mixed, late_mixed, late_grad_mixed, terms = hold(
+            (mixed, grad_mixed, late_mixed, late_grad_mixed, terms)
+        )
+        grad_mixed = swap(grad_mixed, "lon")
+        back = finish(mixed, early)
+        back, grad_mixed = hold((back, grad_mixed))
+        grad_back = finish(grad_mixed, early)
+        late_mixed, back, grad_back = exchange(
+            2, (late_mixed, "lon"), (back, "lat"), (grad_back, "lat")
+        )
+        late_back = finish(late_mixed, table)
+        late_grad_mixed, late_back = exchange(3, (late_grad_mixed, "lon"), (late_back, "lat"))
+        late_grad_back = swap(finish(late_grad_mixed, table), "lat")
+        backs, grad_backs = [back, late_back], [grad_back, late_grad_back]
     summed = lax.psum_scatter(terms, "lat", scatter_dimension=0, tiled=True)
     weight_grad = summed.reshape(-1, degrees_here, 2, total_chan).transpose(1, 2, 0, 3)
     output = (field.astype(f32) + to_grid(backs)).astype(bf16)

time: 805 us -> 727 us (0.903)
  Pallas kernels: 111 us -> 420 us
  waiting for transfers between devices: 402 us -> 139 us
  blocking collectives: 115 us -> 0 us
  starting transfers between devices: 46.7 us -> 29.9 us
    pallas_call x0 -> x4, Pallas kernels: none -> 310 us  [exchange(): pl.pallas_call(lambda *refs: exchange_kernel(axes, *refs), in_specs=[pl.B...]
    all_to_all x11 -> x5, waiting for transfers between devices: 385 us -> 102 us  [swap(): return lax.all_to_all(blocks, axis, split_axis=0, concat_axis=0)]
    all_to_all x3 -> x0, blocking collectives: 115 us -> none  [swap(): return lax.all_to_all(blocks, axis, split_axis=0, concat_axis=0)]
    all_gather x2, waiting for transfers between devices: 16.9 us -> 36.5 us  [on_device(): lax.all_gather(legendre[j * width:(j + 1) * width], 'lon', axis=1, tiled=...]
    all_to_all x11 -> x5, starting transfers between devices: 46.5 us -> 29.8 us  [swap(): return lax.all_to_all(blocks, axis, split_axis=0, concat_axis=0)]
  transfers between devices with their start and end apart: 14 -> 8, of which waited for: 12 -> 6; matrix products, arithmetic and copies ran while one was open for 7% -> 8% of each run, Pallas kernels for 10% -> 46%
where the time goes in v2:
time: 727 us; the launch traced here: 718 us
  Pallas kernels  420 us (58%)
  waiting for transfers between devices  139 us (19%)
  local copies, waits for them, and re-layouts  68.1 us (9%)
  matrix products  42.8 us (6%)
  starting transfers between devices  29.9 us (4%)
  between operations  14 us (2%)
    pallas_call x4, Pallas kernels, exchange(): pl.pallas_call(lambda *refs: exchange_kernel(axes, *refs), in_specs=[pl.B...  310 us
    all_to_all x5, waiting for transfers between devices, swap(): return lax.all_to_all(blocks, axis, split_axis=0, concat_axis=0)  102 us
    pallas_call x4, Pallas kernels, mix(): pl.pallas_call(lambda *refs: mix_kernel(adjoint, *refs), grid=(degrees //...  49 us
    unnamed x66, local copies, waits for them, and re-layouts  48.9 us
    all_gather x2, waiting for transfers between devices, on_device(): lax.all_gather(legendre[j * width:(j + 1) * width], 'lon', axis=1, tiled=...  36.5 us
    all_to_all x5, starting transfers between devices, swap(): return lax.all_to_all(blocks, axis, split_axis=0, concat_axis=0)  29.8 us
    dot_general x2, matrix products, to_grid(): lax.dot_general(got.reshape(total_waves * 2, chan * rows), fourier, (((0,...  21.9 us
    pallas_call x4, Pallas kernels, synthesise(): pl.pallas_call(lambda *refs: synthesise_kernel(chan, *refs), grid=(width...  21.7 us
  transfers between devices with their start and end apart: 8, of which 6 were waited for; matrix products, arithmetic and copies ran while one was open for 8% of the time, Pallas kernels for 46%

profile of v2, /device:TPU:0, one launch (start us, length us, event | category | flops | bytes accessed | tf_op | source)
XLA Modules:
  0.0 718.3 jit_solution(7899224013618938116)
XLA Ops:
  7.2 4.2 fusion
  13.0 10.3 %convolution_convert_fusion = bf16[768,2304]{1,0:T(8,128)(2,1)} fusion(bf16[768,1440]{0,1:T(8,128)(2,1)S(1)} %copy-done.32, bf16[2304,1440]{1,0:T(8,128)(2,1)} %bitcast.32), kind=kOutput, calls=%fused_computation.2 | convolution fusion | flops 5097848832 | bytes 12386304 | tf_op jit(solution)/shard_map/dot_general | solution.py:364
  23.4 5.2 all-to-all-start.1
  28.5 10.6 %convolution_convert_fusion.1 = bf16[768,2304]{1,0:T(8,128)(2,1)} fusion(bf16[768,1440]{0,1:T(8,128)(2,1)} %constant.2.clone, bf16[2304,1440]{1,0:T(8,128)(2,1)} %bitcast.31), kind=kOutput, calls=%fused_computation.3 | convolution fusion | flops 5097848832 | bytes 12386304 | tf_op jit(solution)/shard_map/dot_general | solution.py:364
  39.1 31.5 %all-to-all-done.1.refs_0_ = bf16[8,96,2304]{2,1,0:T(8,128)(2,1)S(1)} async-done(((bf16[8,96,2304]{2,1,0:T(8,128)(2,1)}), bf16[8,96,2304]{2,1,0:T(8,128)(2,1)S(1)}, u32[]{:S(2)}, u32[]{:S(2)}) %all-to-all-start.1) | async-done | bytes 3538976 | tf_op jit(solution)/shard_map/all_to_all | solution.py:24
  70.6 1.8 copy-done.10
  72.4 4.7 all-to-all-start
  77.1 2.0 copy-done.11
  79.1 4.8 shard_map.77.waves_ref
  83.9 35.1 %all-to-all-done.refs_0_ = bf16[8,96,2304]{2,1,0:T(8,128)(2,1)} async-done(((bf16[8,96,2304]{2,1,0:T(8,128)(2,1)}), bf16[8,96,2304]{2,1,0:T(8,128)(2,1)}, u32[]{:S(2)}, u32[]{:S(2)}) %all-to-all-start) | async-done | bytes 3538976 | tf_op jit(solution)/shard_map/all_to_all | solution.py:24
  119.0 6.3 shard_map.76.waves_ref
  125.3 1.8 copy-done.7
  127.1 15.4 %all-gather.5.cloned.1.call-done.table_ref.refs_0_ = bf16[24,384,384]{2,1,0:T(8,128)(2,1)} async-done(((bf16[24,96,384]{2,1,0:T(8,128)(2,1)}), bf16[24,384,384]{2,1,0:T(8,128)(2,1)}) %all-gather.5.cloned.1.call-update) | async-done | bytes 7077904 | tf_op jit(solution)/shard_map/all_gather | solution.py:358
  142.5 3.0 copy-done.4
  145.5 2.0 copy-done.8
  147.5 3.3 shard_map.78.refs_0_
  150.9 1.2 copy-done.14
  152.1 3.4 shard_map.79.refs_1_
  155.4 1.2 copy-done.15
  156.6 137.7 %shard_map.80 = (bf16[4,96,2304]{2,1,0:T(8,128)(2,1)}, bf16[4,96,2304]{2,1,0:T(8,128)(2,1)}) custom-call(bf16[4,96,2304]{2,1,0:T(8,128)(2,1)} %copy-done.14, bf16[4,96,2304]{2,1,0:T(8,128)(2,1)} %copy-done.15), custom_call_target="tpu_custom_call" | custom-call | bytes 113246208 | tf_op jit(solution)/shard_map/pallas_call | solution.py:77
  294.4 1.5 copy-done.26
  295.8 13.1 %shard_map.81 = (bf16[4,96,2304]{2,1,0:T(8,128)(2,1)}, bf16[96,48,192]{2,1,0:T(8,128)(2,1)S(1)}) custom-call(bf16[4,96,2304]{2,1,0:T(8,128)(2,1)S(1)} %copy-done.26, bf16[96,2,192,192]{3,2,1,0:T(8,128)(2,1)} %refs_1_.7), custom_call_target="tpu_custom_call" | custom-call | flops 679477248 | bytes 19464192 | tf_op jit(solution)/shard_map/pallas_call | solution.py:280
  309.0 1.4 copy-done.19
  310.4 11.8 %shard_map.82 = (bf16[4,96,2304]{2,1,0:T(8,128)(2,1)S(1)}, bf16[96,48,192]{2,1,0:T(8,128)(2,1)S(1)}) custom-call(bf16[4,96,2304]{2,1,0:T(8,128)(2,1)S(1)} %copy-done.25, bf16[96,2,192,192]{3,2,1,0:T(8,128)(2,1)} %refs_1_.7), custom_call_target="tpu_custom_call" | custom-call | flops 679477248 | bytes 19464192 | tf_op jit(solution)/shard_map/pallas_call | solution.py:280
  322.2 1.4 copy-done.21
  323.6 1.2 copy-done.27
  324.8 21.1 %all-gather.3.cloned.1.call-done.table_ref.refs_0_ = bf16[24,384,384]{2,1,0:T(8,128)(2,1)} async-done(((bf16[24,96,384]{2,1,0:T(8,128)(2,1)}), bf16[24,384,384]{2,1,0:T(8,128)(2,1)}) %all-gather.3.cloned.1.call-update) | async-done | bytes 7077904 | tf_op jit(solution)/shard_map/all_gather | solution.py:358
  345.9 3.0 copy-done
  348.9 3.4 shard_map.84.refs_1_
  352.3 1.2 copy-done.12
  353.5 3.4 shard_map.83.refs_0_
  356.9 1.2 copy-done.13
  358.1 81.9 %shard_map.85 = (bf16[4,96,2304]{2,1,0:T(8,128)(2,1)}, bf16[4,96,2304]{2,1,0:T(8,128)(2,1)}) custom-call(bf16[4,96,2304]{2,1,0:T(8,128)(2,1)} %copy-done.13, bf16[4,96,2304]{2,1,0:T(8,128)(2,1)} %copy-done.12), custom_call_target="tpu_custom_call" | custom-call | bytes 113246208 | tf_op jit(solution)/shard_map/pallas_call | solution.py:77
  440.0 10.3 %all-to-all-start.2 = ((bf16[4,96,2304]{2,1,0:T(8,128)(2,1)}), bf16[4,96,2304]{2,1,0:T(8,128)(2,1)S(1)}, u32[]{:S(2)}, u32[]{:S(2)}) async-start(bf16[4,96,2304]{2,1,0:T(8,128)(2,1)} %get-tuple-element.49), calls=%async_computation.2 | async-start | bytes 3538944 | tf_op jit(solution)/shard_map/all_to_all | solution.py:24
  450.3 1.6 copy-done.24
  451.9 12.1 %shard_map.86 = (bf16[4,96,2304]{2,1,0:T(8,128)(2,1)S(1)}, bf16[96,48,192]{2,1,0:T(8,128)(2,1)S(1)}) custom-call(bf16[4,96,2304]{2,1,0:T(8,128)(2,1)S(1)} %copy-done.24, bf16[96,2,192,192]{3,2,1,0:T(8,128)(2,1)} %refs_1_.7), custom_call_target="tpu_custom_call" | custom-call | flops 679477248 | bytes 19464192 | tf_op jit(solution)/shard_map/pallas_call | solution.py:280
  464.0 1.2 copy-done.29
  465.2 11.9 %shard_map.87 = (bf16[4,96,2304]{2,1,0:T(8,128)(2,1)S(1)}, bf16[96,48,192]{2,1,0:T(8,128)(2,1)S(1)}) custom-call(bf16[4,96,2304]{2,1,0:T(8,128)(2,1)S(1)} %copy-done.23, bf16[96,2,192,192]{3,2,1,0:T(8,128)(2,1)} %refs_1_.7), custom_call_target="tpu_custom_call" | custom-call | flops 679477248 | bytes 19464192 | tf_op jit(solution)/shard_map/pallas_call | solution.py:280
  477.2 1.2 copy-done.28
  478.4 14.4 %shard_map.88 = bf16[192,36864]{1,0:T(8,128)(2,1)} custom-call(bf16[96,48,192]{2,1,0:T(8,128)(2,1)S(1)} %copy-done.20, bf16[96,48,192]{2,1,0:T(8,128)(2,1)S(1)} %get-tuple-element.56.refs_1_, bf16[96,48,192]{2,1,0:T(8,128)(2,1)S(1)} %copy-done.22, bf16[96,48,192]{2,1,0:T(8,128)(2,1)S(1)} %get-tuple-element.58.refs_3_), custom_call_target="tpu_custom_call" | custom-call | flops 1358954496 | bytes 21233664 | tf_op jit(solution)/shard_map/pallas_call | solution.py:328
  492.8 5.1 all-to-all-start.3
  497.9 4.2 copy-done.5
  502.1 5.2 shard_map.89.refs_1_
  508.6 29.2 %all-to-all-done.3.refs_1_ = bf16[4,96,2304]{2,1,0:T(8,128)(2,1)S(1)} async-done(((bf16[4,96,2304]{2,1,0:T(8,128)(2,1)}), bf16[4,96,2304]{2,1,0:T(8,128)(2,1)S(1)}, u32[]{:S(2)}, u32[]{:S(2)}) %all-to-all-start.3) | async-done | bytes 1769504 | tf_op jit(solution)/shard_map/all_to_all | solution.py:24
  537.8 3.4 copy-done.6
  541.1 5.2 shard_map.90.refs_2_
  547.6 56.1 %shard_map.91 = (bf16[4,96,2304]{2,1,0:T(8,128)(2,1)}, bf16[8,48,2304]{2,1,0:T(8,128)(2,1)}, bf16[8,48,2304]{2,1,0:T(8,128)(2,1)}) custom-call(bf16[4,96,2304]{2,1,0:T(8,128)(2,1)} %copy-done.29, bf16[8,48,2304]{2,1,0:T(8,128)(2,1)} %copy-done.17, bf16[8,48,2304]{2,1,0:T(8,128)(2,1)} %copy-done.18), custom_call_target="tpu_custom_call" | custom-call | bytes 169869312 | tf_op jit(solution)/shard_map/pallas_call | solution.py:77
  603.7 3.0 copy-done.2
  606.7 1.5 copy-done.30
  608.2 5.2 shard_map.92.refs_1_
  614.6 34.5 %shard_map.93 = (bf16[4,96,2304]{2,1,0:T(8,128)(2,1)}, bf16[8,48,2304]{2,1,0:T(8,128)(2,1)}) custom-call(bf16[4,96,2304]{2,1,0:T(8,128)(2,1)} %copy-done.28, bf16[8,48,2304]{2,1,0:T(8,128)(2,1)} %copy-done.16), custom_call_target="tpu_custom_call" | custom-call | bytes 113246208 | tf_op jit(solution)/shard_map/pallas_call | solution.py:77
  649.2 3.0 copy-done.3
  652.2 1.5 copy-done.31
  653.7 6.0 shard_map.94
  659.7 4.6 all-to-all-start.4
  664.3 2.2 pad_maximum_fusion
  666.5 3.6 copy.8
  670.1 10.9 %add_convert_fusion.1 = bf16[48,48,1440]{2,1,0:T(8,128)(2,1)} fusion(bf16[48,48,1440]{2,1,0:T(8,128)(2,1)} %param.5, bf16[48,48,768]{2,1,0:T(8,128)(2,1)} %bitcast.29, bf16[768,1440,1]{0,1,2:T(8,128)(2,1)} %constant.3), kind=kOutput, calls=%fused_computation.1 | convolution fusion | flops 5106032640 | bytes 19021824 | tf_op jit(solution)/shard_map/dot_general | solution.py:370
  681.0 6.1 all-to-all-done.4
  687.1 2.2 pad_maximum_fusion.1
  689.4 3.6 copy.9
  693.0 10.9 %add_convert_fusion = bf16[48,48,1440]{2,1,0:T(8,128)(2,1)} fusion(bf16[48,48,1440]{2,1,0:T(8,128)(2,1)} %param.6, bf16[48,48,768]{2,1,0:T(8,128)(2,1)} %bitcast.28, bf16[768,1440,1]{0,1,2:T(8,128)(2,1)} %constant.3), kind=kOutput, calls=%fused_computation | convolution fusion | flops 5106032640 | bytes 19021824 | tf_op jit(solution)/shard_map/dot_general | solution.py:370
  703.9 3.9 reshape.37
  707.9 3.9 copy.12
  (51 shorter events, 5.3 us)
Async XLA Ops:
  7.2 135.3 %all-gather.5.cloned.1.call-start = ((), (), s32[]{:S(2)}) async-start(), calls=%async_computation.7 | async-start | bytes 8847360 | tf_op jit(solution)/shard_map/all_gather | solution.py:358
  11.4 1.6 copy-start.32
  11.4 334.5 %all-gather.3.cloned.1.call-start = ((), (), s32[]{:S(2)}) async-start(), calls=%async_computation.6 | async-start | bytes 8847360 | tf_op jit(solution)/shard_map/all_gather | solution.py:358
  23.4 47.3 %all-to-all-start.1 = ((bf16[8,96,2304]{2,1,0:T(8,128)(2,1)}), bf16[8,96,2304]{2,1,0:T(8,128)(2,1)S(1)}, u32[]{:S(2)}, u32[]{:S(2)}) async-start(bf16[8,96,2304]{2,1,0:T(8,128)(2,1)} %bitcast.27), calls=%async_computation.1 | async-start | bytes 7077888 | tf_op jit(solution)/shard_map/all_to_all | solution.py:24
  70.6 1.8 copy-start.10
  72.4 46.6 %all-to-all-start = ((bf16[8,96,2304]{2,1,0:T(8,128)(2,1)}), bf16[8,96,2304]{2,1,0:T(8,128)(2,1)}, u32[]{:S(2)}, u32[]{:S(2)}) async-start(bf16[8,96,2304]{2,1,0:T(8,128)(2,1)} %bitcast.26), calls=%async_computation | async-start | bytes 7077888 | tf_op jit(solution)/shard_map/all_to_all | solution.py:24
  77.1 2.0 copy-start.11
  125.3 1.8 copy-start.7
  142.5 3.0 copy-start.4
  145.5 2.0 copy-start.8
  150.9 1.2 copy-start.14
  155.4 1.2 copy-start.15
  294.3 1.5 copy-start.26
  295.8 14.6 %copy-start.25 = (bf16[4,96,2304]{2,1,0:T(8,128)(2,1)S(1)}, bf16[4,96,2304]{2,1,0:T(8,128)(2,1)}, u32[]{:S(2)}) copy-start(bf16[4,96,2304]{2,1,0:T(8,128)(2,1)} %get-tuple-element.42.refs_0_) | copy-start | bytes 5308420
  309.0 1.4 copy-start.19
  322.2 1.4 copy-start.21
  323.6 1.2 copy-start.27
  345.9 3.0 copy-start
  348.9 4.6 copy-start.1
  348.9 4.6 copy-start.9
  352.3 1.2 copy-start.12
  356.9 1.2 copy-start.13
  440.0 52.8 %all-to-all-start.2 = ((bf16[4,96,2304]{2,1,0:T(8,128)(2,1)}), bf16[4,96,2304]{2,1,0:T(8,128)(2,1)S(1)}, u32[]{:S(2)}, u32[]{:S(2)}) async-start(bf16[4,96,2304]{2,1,0:T(8,128)(2,1)} %get-tuple-element.49), calls=%async_computation.2 | async-start | bytes 3538944 | tf_op jit(solution)/shard_map/all_to_all | solution.py:24
  450.3 14.9 %copy-start.23 = (bf16[4,96,2304]{2,1,0:T(8,128)(2,1)S(1)}, bf16[4,96,2304]{2,1,0:T(8,128)(2,1)}, u32[]{:S(2)}) copy-start(bf16[4,96,2304]{2,1,0:T(8,128)(2,1)} %get-tuple-element.53.refs_0_) | copy-start | bytes 5308420
  450.3 253.6 %reduce-scatter.2.cloned.1.call-start = ((), (), s32[]{:S(2)}) async-start(), calls=%async_computation.8 | async-start | bytes 15925248 | tf_op jit(solution)/shard_map/reduce_scatter | solution.py:429
  450.3 1.6 copy-start.24
  464.0 1.2 copy-start.29
  465.2 13.2 %copy-start.20 = (bf16[96,48,192]{2,1,0:T(8,128)(2,1)S(1)}, bf16[96,48,192]{2,1,0:T(8,128)(2,1)}, u32[]{:S(2)}) copy-start(bf16[96,48,192]{2,1,0:T(8,128)(2,1)} %copy-done.19) | copy-start | bytes 5308420
  465.2 13.2 %copy-start.22 = (bf16[96,48,192]{2,1,0:T(8,128)(2,1)S(1)}, bf16[96,48,192]{2,1,0:T(8,128)(2,1)}, u32[]{:S(2)}) copy-start(bf16[96,48,192]{2,1,0:T(8,128)(2,1)} %copy-done.21) | copy-start | bytes 5308420
  477.2 1.2 copy-start.28
  492.8 45.0 %all-to-all-start.3 = ((bf16[4,96,2304]{2,1,0:T(8,128)(2,1)}), bf16[4,96,2304]{2,1,0:T(8,128)(2,1)S(1)}, u32[]{:S(2)}, u32[]{:S(2)}) async-start(bf16[4,96,2304]{2,1,0:T(8,128)(2,1)} %copy-done.27), calls=%async_computation.3 | async-start | bytes 3538944 | tf_op jit(solution)/shard_map/all_to_all | solution.py:24
  497.9 4.2 copy-start.5
  507.3 1.2 copy-start.17
  537.8 3.4 copy-start.6
  546.4 1.2 copy-start.18
  603.7 3.0 copy-start.2
  606.7 1.5 copy-start.30
  613.4 1.2 copy-start.16
  649.2 3.0 copy-start.3
  652.2 1.5 copy-start.31
  659.7 27.5 %all-to-all-start.4 = ((bf16[8,48,2304]{2,1,0:T(8,128)(2,1)}), bf16[8,48,2304]{2,1,0:T(8,128)(2,1)}, u32[]{:S(2)}, u32[]{:S(2)}) async-start(bf16[8,48,2304]{2,1,0:T(8,128)(2,1)} %shard_map.94), calls=%async_computation.4 | async-start | bytes 3538944 | tf_op jit(solution)/shard_map/all_to_all | solution.py:24
Sparse Core Ops, SparseCore 0:
  11.6 130.8 all-gather.4
  144.1 201.7 all-gather.2
  492.9 142.3 reduce-scatter.1
